TPU v7x, 128 devices: a whole 4x4x4 slice. The times are simulated.
128 devices in a mesh: section: 8 (over y, core), dp: 16 (over x, z).
Axes of the slice: x: 4, y: 4, z: 4, core: 2. Of those that a mesh axis runs over, the one named last changes fastest.
Arguments:
- activations: bfloat16 [196608, 8192], P(('section', 'dp')), parts along dimension 0, may hold values from -36 to 36, as said below
- cotangent: bfloat16 [196608, 512], P(('section', 'dp')), parts along dimension 0, may hold values from -16 to 16, as said below
- weight: bfloat16 [65536, 512], P(('section', 'dp')), parts along dimension 0, may hold values from -0.0625 to 0.0625
- row_state: float32 [65536], P(('section', 'dp')), parts along dimension 0, may hold values from 81 to 7372800, as said below
- column_state: float32 [4096], P('section'), parts along dimension 0, may hold values from 307 to 835584, as said below
Outputs:
- new_weight: bfloat16 [65536, 512], P('section'), parts along dimension 0
- row_moment: float32 [65536], P(('section', 'dp')), parts along dimension 0
- column_moment: float32 [4096], P('section'), parts along dimension 0
There are 8 independent parts, one for each index of `section`. A program takes and returns all parts, laid end to end along the dimension named above; each array names one. Nothing has to cross between parts.
Inputs may be any that keep to these rules, and one draw needn't show every extreme that they name: activations are finite. cotangent entries are finite. `row_state`: positive. `column_state`: positive.
All inputs are finite; a program needn't handle non-finite values.
Results may differ from a plain program's by a relative error of at most 0.017.
Values may be sent and summed in bfloat16 or wider, within the bound.
A program may use at most 128 MiB of HBM per device.

v0:
```python
import jax
import jax.numpy as jnp
from jax import lax
from jax.sharding import PartitionSpec as P

decay_rate = 0.8
learn_rate = 0.1
clip_level = 1.0
epsilon_one = 1e-30


def direction(gradient, row_moment, column_moment, mean_row):
    return gradient / jnp.sqrt(row_moment[:, None] * column_moment[None, :] / mean_row)


def apply_step(weight, update, square_mean):
    ratio = jnp.sqrt(square_mean) / clip_level
    fresh = weight.astype(jnp.float32) - learn_rate * update / jnp.maximum(1.0, ratio)
    return fresh.astype(jnp.bfloat16)


def local(activations, cotangent, weight, row_state, column_state):
    local_rows = weight.shape[0]
    columns = weight.shape[1]
    total_rows = local_rows * lax.axis_size("dp")
    gradient = lax.psum_scatter(
        lax.dot_general(
            activations, cotangent, (((0,), (0,)), ((), ())), preferred_element_type=jnp.float32
        ).astype(jnp.bfloat16),
        "dp",
        scatter_dimension=0,
        tiled=True,
    ).astype(jnp.float32)
    squares = gradient * gradient + epsilon_one
    row_moment = decay_rate * row_state + (1.0 - decay_rate) * jnp.mean(squares, axis=1)
    column_part = jnp.sum(squares, axis=0)
    row_part = jnp.sum(row_moment)
    column_sum, row_sum = lax.psum((column_part, row_part), "dp")
    column_moment = decay_rate * column_state + (1.0 - decay_rate) * column_sum / total_rows
    mean_row = row_sum / total_rows
    update = direction(gradient, row_moment, column_moment, mean_row)
    square_mean = lax.psum(jnp.sum(update * update), "dp") / (total_rows * columns)
    fresh = apply_step(weight, update, square_mean)
    new_weight = lax.all_gather(fresh, "dp", axis=0, tiled=True)
    return (new_weight, row_moment, column_moment)


def solution(mesh):
    in_specs = (
        P(("section", "dp"), None),
        P(("section", "dp"), None),
        P(("section", "dp"), None),
        P(("section", "dp")),
        P("section"),
    )
    out_specs = (P("section", None), P(("section", "dp")), P("section"))
    return jax.shard_map(local, mesh=mesh, in_specs=in_specs, out_specs=out_specs, check_vma=False)
```

profile of v0, /device:TPU:0, one launch (start us, length us, event | category | flops | bytes accessed | tf_op | source)
XLA Modules:
  0.0 281.8 jit_solution(11852893945546862672)
XLA Ops:
  7.2 0.0 copy-start
  7.2 0.0 reduce-scatter.2.cloned.1.call-start
  7.2 1.4 copy-done
  8.6 20.1 %convolution_convert_fusion = bf16[8192,512]{1,0:T(8,128)(2,1)} fusion(bf16[1536,8192]{1,0:T(8,128)(2,1)} %param.5, bf16[1536,512]{1,0:T(8,128)(2,1)S(1)} %copy-done), kind=kOutput, calls=%fused_computation | convolution fusion | flops 12889096192 | bytes 35127296 | tf_op jit(solution)/shard_map/dot_general | solution.py:27
  28.7 0.0 copy-start.5
  28.7 0.0 copy-start.4
  28.7 0.0 copy-start.1
  28.7 0.0 reduce-scatter.2.cloned.1.call-update
  28.7 0.0 all-gather.2.cloned.1.call-start
  28.8 87.6 %reduce-scatter.2.cloned.1.call-done = bf16[512,512]{1,0:T(8,128)(2,1)} async-done(((bf16[8192,512]{1,0:T(8,128)(2,1)}), bf16[512,512]{1,0:T(8,128)(2,1)}) %reduce-scatter.2.cloned.1.call-update) | async-done | bytes 524304 | tf_op jit(solution)/shard_map/reduce_scatter | solution.py:26
  116.4 1.3 fusion.1
  117.7 0.0 copy-done.5
  117.7 0.6 fusion.3
  118.3 0.0 copy-start.3
  118.3 38.8 %all-reduce = (f32[]{:T(128)}, f32[512]{0:T(512)S(1)}) all-reduce(f32[]{:T(128)} %get-tuple-element.7, f32[512]{0:T(512)S(1)} %get-tuple-element.3), channel_id=1, replica_groups=mesh['section'=8,'dp'=16] {'dp'}, use_global_device_ids=true, to_apply=%region_5.0 | all-reduce | flops 513 | bytes 4104 | tf_op jit(solution)/shard_map/psum | solution.py:38
  157.7 0.0 copy-done.4
  157.7 0.0 copy-start.2
  157.7 2.1 multiply_reduce_fusion
  159.9 36.1 %psum.23 = f32[]{:T(128)} all-reduce(f32[]{:T(128)} %multiply_reduce_fusion), channel_id=1, replica_groups=mesh['section'=8,'dp'=16] {'dp'}, use_global_device_ids=true, to_apply=%region_7.0 | all-reduce | flops 1 | bytes 8 | tf_op jit(solution)/shard_map/psum | solution.py:42
  196.6 0.0 copy-done.1
  196.6 2.2 subtract_convert_fusion
  198.9 0.0 all-gather.2.cloned.1.call-update
  198.9 68.7 %all-gather.2.cloned.1.call-done = bf16[8192,512]{1,0:T(8,128)(2,1)} async-done(((bf16[512,512]{1,0:T(8,128)(2,1)}), bf16[8192,512]{1,0:T(8,128)(2,1)}) %all-gather.2.cloned.1.call-update) | async-done | bytes 8388624 | tf_op jit(solution)/shard_map/all_gather | solution.py:44
  267.6 7.3 %copy.9 = bf16[8192,512]{1,0:T(8,128)(2,1)} copy(bf16[8192,512]{1,0:T(8,128)(2,1)} %all-gather.2.cloned.1.call-done) | data formatting | bytes 16777216
  274.9 0.0 copy-done.3
  274.9 0.0 copy-done.2
  (1 shorter events, 0.0 us)
Async XLA Ops:
  7.2 1.4 copy-start
  7.2 109.2 %reduce-scatter.2.cloned.1.call-start = ((), (), s32[]{:S(2)}) async-start(), calls=%async_computation.1 | async-start | bytes 8912896 | tf_op jit(solution)/shard_map/reduce_scatter | solution.py:26
  28.7 89.0 %copy-start.5 = (f32[512]{0:T(512)S(1)}, f32[512]{0:T(512)}, u32[]{:S(2)}) copy-start(f32[512]{0:T(512)} %param.8) | copy-start | bytes 6148
  28.7 129.0 %copy-start.4 = (f32[512]{0:T(512)S(1)}, f32[512]{0:T(512)}, u32[]{:S(2)}) copy-start(f32[512]{0:T(512)} %param.9) | copy-start | bytes 6148
  28.7 167.9 %copy-start.1 = (bf16[512,512]{1,0:T(8,128)(2,1)S(1)}, bf16[512,512]{1,0:T(8,128)(2,1)}, u32[]{:S(2)}) copy-start(bf16[512,512]{1,0:T(8,128)(2,1)} %param.7) | copy-start | bytes 1572868
  28.7 238.9 %all-gather.2.cloned.1.call-start = ((), (), s32[]{:S(2)}) async-start(), calls=%async_computation.2 | async-start | bytes 8912896 | tf_op jit(solution)/shard_map/all_gather | solution.py:44
  118.3 156.6 %copy-start.3 = (f32[512]{0:T(512)}, f32[512]{0:T(512)S(1)}, u32[]{:S(2)}) copy-start(f32[512]{0:T(512)S(1)} %get-tuple-element.13) | copy-start | bytes 6148
  157.7 117.2 %copy-start.2 = (f32[512]{0:T(512)}, f32[512]{0:T(512)S(1)}, u32[]{:S(2)}) copy-start(f32[512]{0:T(512)S(1)} %multiply_add_fusion) | copy-start | bytes 6148
Sparse Core Ops, SparseCore 0:
  28.9 87.4 reduce-scatter.1
  199.0 68.5 all-gather.1
where the time goes:
time: 283 us; the launch traced here: 282 us
  waiting for transfers between devices  156 us (55%)
  blocking collectives  74.8 us (26%)
  matrix products  20.1 us (7%)
  between operations  15.4 us (5%)
  local copies, waits for them, and re-layouts  8.7 us (3%)
  other arithmetic  6.27 us (2%)
    reduce_scatter x1, waiting for transfers between devices, local(): lax.psum_scatter(lax.dot_general(activations, cotangent, (((0,), (0,)), (...  87.6 us
    all_gather x1, waiting for transfers between devices, local(): new_weight = lax.all_gather(fresh, 'dp', axis=0, tiled=True)  68.7 us
    psum x1, blocking collectives, local(): column_sum, row_sum = lax.psum((column_part, row_part), 'dp')  38.8 us
    psum x1, blocking collectives, local(): lax.psum(jnp.sum(update * update), 'dp') / (total_rows * columns)  36.1 us
    dot_general x1, matrix products, local(): lax.dot_general(activations, cotangent, (((0,), (0,)), ((), ())), preferr...  20.1 us
    unnamed x13, local copies, waits for them, and re-layouts  8.7 us
  transfers between devices with their start and end apart: 2, of which 2 were waited for; matrix products, arithmetic and copies ran while one was open for 0% of the time, Pallas kernels for 0%

commit v1 on v0

v1 whole, which is shorter than its diff:
```python
import functools

import jax
import jax.numpy as jnp
from jax import lax
from jax.experimental import pallas as pl
from jax.experimental.pallas import tpu as pltpu
from jax.sharding import PartitionSpec as P

MESH = pl.DeviceIdType.MESH
decay_rate = 0.8
learn_rate = 0.1
clip_level = 1.0
epsilon_one = 1e-30
SIDE = 4
FAR, NEXT, LAST, OWN = 0, 1, 2, 3
SLOTS = 3
F32 = jnp.float32
BF16 = jnp.bfloat16


def offset(k):
    return 2 - k + (k // 2) * (7 - 2 * k)


def kernel(
    act, cot, weight, row_state, col_state,
    out, row_out, col_out,
    abuf, cbuf, wbuf, grad, r1, r2, norm, fresh, msg, heard,
    a_sem, c_sem, w_sem, o_sem,
    s1, v1, s2, v2, ss, vs, g1s, g1v, f1s, f1v, g2s, g2v, f2s, f2v,
):
    me = lax.axis_index("dp")
    px, pz = me // SIDE, me % SIDE
    n = SIDE * SIDE
    q, ff = grad.shape[4], grad.shape[5]
    shard = 4 * q
    lanes = ff // 128

    def place(g, da, db):
        dx, dz = (da, db) if g == 0 else (db, da)
        return ((px + dx) % SIDE) * SIDE + (pz + dz) % SIDE

    def send(src, dst, ssem, rsem, target):
        return pltpu.make_async_remote_copy(
            src_ref=src, dst_ref=dst, send_sem=ssem, recv_sem=rsem,
            device_id={"dp": target}, device_id_type=MESH,
        )

    step = (1, SIDE - 1)

    def fetch(i, g):
        k, m = i // SIDE, i % SIDE
        col = place(g, offset(k), offset(m)) * shard + g * 2 * q
        return pltpu.make_async_copy(
            act.at[:, pl.ds(pl.multiple_of(col, 2 * q), 2 * q)],
            abuf.at[i % SLOTS, g], a_sem.at[i % SLOTS, g],
        )

    barrier = pltpu.get_barrier_semaphore()
    for j in range(1, n):
        pl.semaphore_signal(
            barrier, inc=1, device_id={"dp": (me + j) % n}, device_id_type=MESH
        )
    get_cot = pltpu.make_async_copy(cot, cbuf, c_sem)
    get_cot.start()
    for i in range(SLOTS - 1):
        for g in range(2):
            fetch(i, g).start()
    get_weight = pltpu.make_async_copy(weight, wbuf, w_sem)
    get_weight.start()
    get_cot.wait()

    def far1(g, d, m):
        return send(grad.at[g, FAR, m, d], r1.at[0, g, d, m],
                    s1.at[0, g, d, m], v1.at[0, g, d, m], place(g, step[d], 0))

    def near1(g, d, m):
        return send(grad.at[g, NEXT + d, m, 1 - d], r1.at[1, g, d, m],
                    s1.at[1, g, d, m], v1.at[1, g, d, m], place(g, step[d], 0))

    def both1(g, d, m):
        return send(grad.at[g, NEXT + d, m, d], r1.at[2, g, d, m],
                    s1.at[2, g, d, m], v1.at[2, g, d, m], place(g, step[d], 0))

    @pl.loop(0, SIDE * SIDE)
    def _(i):
        k, m = i // SIDE, i % SIDE
        for g in range(2):
            fetch(i, g).wait()

            @pl.when(i + SLOTS - 1 < SIDE * SIDE)
            def _():
                fetch(i + SLOTS - 1, g).start()

            part = lax.dot_general(
                abuf[i % SLOTS, g], cbuf[...], (((0,), (0,)), ((), ())),
                preferred_element_type=F32,
            ).astype(BF16)
            grad[g, k, m, 0] = part[:q]
            grad[g, k, m, 1] = part[q:]

        @pl.when(i == 0)
        def _():
            pl.semaphore_wait(barrier, n - 1)

        @pl.when(k == FAR)
        def _():
            for g in range(2):
                for d in range(2):
                    far1(g, d, m).start()

        @pl.when(k == NEXT)
        def _():
            for g in range(2):
                near1(g, 0, m).start()

        @pl.when(k == LAST)
        def _():
            for g in range(2):
                near1(g, 1, m).start()

    @pl.loop(0, SIDE)
    def _(m):
        for g in range(2):
            for d in range(2):
                far1(g, d, m).wait_recv()
                grad[g, NEXT + d, m, d] = (
                    grad[g, NEXT + d, m, d].astype(F32) + r1[0, g, d, m].astype(F32)
                ).astype(BF16)
                both1(g, d, m).start()

    def total1(g, m, h):
        both1(g, h, m).wait_recv()
        near1(g, 1 - h, m).wait_recv()
        return (
            grad[g, OWN, m, h].astype(F32) + r1[2, g, h, m].astype(F32)
        ) + r1[1, g, 1 - h, m].astype(F32)

    def far2(g, d):
        return send(grad.at[g, OWN, FAR, d], r2.at[0, g, d],
                    s2.at[0, g, d], v2.at[0, g, d], place(g, 0, step[d]))

    def near2(g, d):
        return send(grad.at[g, OWN, NEXT + d, 1 - d], r2.at[1, g, d],
                    s2.at[1, g, d], v2.at[1, g, d], place(g, 0, step[d]))

    def both2(g, d):
        return send(grad.at[g, OWN, NEXT + d, d], r2.at[2, g, d],
                    s2.at[2, g, d], v2.at[2, g, d], place(g, 0, step[d]))

    for g in range(2):
        for h in range(2):
            grad[g, OWN, FAR, h] = total1(g, FAR, h).astype(BF16)
            far2(g, h).start()
    for d in range(2):
        for g in range(2):
            for h in range(2):
                grad[g, OWN, NEXT + d, h] = total1(g, NEXT + d, h).astype(BF16)
            near2(g, d).start()
    for d in range(2):
        for g in range(2):
            far2(g, d).wait_recv()
            grad[g, OWN, NEXT + d, d] = (
                grad[g, OWN, NEXT + d, d].astype(F32) + r2[0, g, d].astype(F32)
            ).astype(BF16)
            both2(g, d).start()

    eye = lax.broadcasted_iota(jnp.int32, (q, q), 0) == lax.broadcasted_iota(jnp.int32, (q, q), 1)
    square_sum = jnp.zeros((1, ff), F32)
    update_sum = jnp.zeros((1, ff), F32)
    row_sum = jnp.zeros((1, 1), F32)
    for g in range(2):
        for h in range(2):
            i = 2 * g + h
            mine = total1(g, OWN, h)
            both2(g, h).wait_recv()
            near2(g, 1 - h).wait_recv()
            mine = (mine + r2[2, g, h].astype(F32)) + r2[1, g, 1 - h].astype(F32)
            squares = mine * mine + epsilon_one
            state = jnp.sum(jnp.where(eye, row_state[i:i + 1, :], 0.0), axis=1, keepdims=True)
            moment = decay_rate * state + (1.0 - decay_rate) * (
                jnp.sum(squares, axis=1, keepdims=True) / ff
            )
            row_out[i:i + 1, :] = jnp.sum(jnp.where(eye, moment, 0.0), axis=0, keepdims=True)
            scaled = mine * lax.rsqrt(moment)
            norm[i] = scaled
            square_sum += jnp.sum(squares, axis=0, keepdims=True)
            update_sum += jnp.sum(scaled * scaled, axis=0, keepdims=True)
            row_sum += jnp.sum(moment, axis=0, keepdims=True)
    msg[...] = jnp.zeros(msg.shape, F32)
    for j in range(lanes):
        msg[j:j + 1, :] = square_sum[:, 128 * j:128 * (j + 1)]
        msg[lanes + j:lanes + j + 1, :] = update_sum[:, 128 * j:128 * (j + 1)]
    msg[2 * lanes:2 * lanes + 1, :] = jnp.broadcast_to(row_sum, (1, 128))

    def tell(j):
        return send(msg, heard.at[me], ss.at[j], vs.at[me], (me + j) % n)

    def hear(j):
        other = (me + j) % n
        return send(msg, heard.at[other], ss.at[0], vs.at[other], other)

    for j in range(1, n):
        tell(j).start()
    heard[me] = msg[...]
    for j in range(1, n):
        hear(j).wait_recv()
    total = heard[0]
    for j in range(1, n):
        total = total + heard[j]
    col_moment = decay_rate * col_state[...] + (1.0 - decay_rate) * (total[:lanes] / (n * shard))
    col_out[...] = col_moment
    mean_row = jnp.max(total[2 * lanes:2 * lanes + 1], axis=1, keepdims=True) / (n * shard)
    update_mean = (
        jnp.sum(jnp.sum(total[lanes:2 * lanes] / col_moment, axis=1, keepdims=True), axis=0, keepdims=True)
        * mean_row / (n * shard * ff)
    )
    ratio = jnp.sqrt(update_mean) / clip_level
    factor = lax.rsqrt(col_moment) * (learn_rate * jnp.sqrt(mean_row) / jnp.maximum(1.0, ratio))

    def rows(dev, g, h):
        return out.at[pl.ds(pl.multiple_of(dev * shard + (2 * g + h) * q, q), q)]

    def own1(g, d, h):
        return send(fresh.at[2 * g + h], rows(me, g, h),
                    g1s.at[g, d, h], g1v.at[g, d, h], place(g, 0, step[d]))

    def own2(g, d, h):
        return send(fresh.at[2 * g + h], rows(me, g, h),
                    g2s.at[g, d, 0, h], g2v.at[g, d, 0, h], place(g, step[d], 0))

    def pass1(g, d):
        block = rows(place(g, 0, step[1 - d]), g, d)
        return send(block, block, f1s.at[g, d], f1v.at[g, d], place(g, 0, step[d]))

    away = (0, 1, 3, 2)

    def line2(g, d, e, h):
        block = rows(place(g, 0, away[e]), g, h)
        return send(block, block, g2s.at[g, d, e, h], g2v.at[g, d, e, h], place(g, step[d], 0))

    def pass2(g, d, e):
        block = rows(place(g, step[1 - d], away[e]), g, d)
        return send(block, block, f2s.at[g, d, e], f2v.at[g, d, e], place(g, step[d], 0))

    keep = []
    get_weight.wait()
    for h in range(2):
        for g in range(2):
            i = 2 * g + h
            for j in range(lanes):
                at = slice(128 * j, 128 * (j + 1))
                fresh[i, :, at] = (
                    wbuf[i * q:(i + 1) * q, at].astype(F32) - norm[i, :, at] * factor[j:j + 1]
                ).astype(BF16)
            own1(g, 0, h).start()
            own1(g, 1, h).start()
            own2(g, 0, h).start()
            own2(g, 1, h).start()
            keep.append(pltpu.make_async_copy(fresh.at[i], rows(me, g, h), o_sem.at[i]))
            keep[-1].start()
    for h in range(2):
        for g in range(2):
            for d in range(2):
                own1(g, 1 - d, h).wait_recv()
                if h == 1 - d:
                    pass1(g, 1 - d).start()
                line2(g, 0, 1 + d, h).start()
                line2(g, 1, 1 + d, h).start()
    for e in (0, 1, 2, 3):
        if e == 3:
            for g in range(2):
                for h in range(2):
                    pass1(g, h).wait_recv()
                    line2(g, 0, 3, h).start()
                    line2(g, 1, 3, h).start()
        for g in range(2):
            for d in range(2):
                if e == 0:
                    own2(g, d, d).wait_recv()
                else:
                    line2(g, d, e, d).wait_recv()
                pass2(g, d, e).start()

    for e in range(4):
        for g in range(2):
            for d in range(2):
                (own2(g, d, 1 - d) if e == 0 else line2(g, d, e, 1 - d)).wait_recv()
                pass2(g, d, e).wait_recv()
    for copy in keep:
        copy.wait()
    for g in range(2):
        for d in range(2):
            for m in range(SIDE):
                far1(g, d, m).wait_send()
                near1(g, d, m).wait_send()
                both1(g, d, m).wait_send()
            far2(g, d).wait_send()
            near2(g, d).wait_send()
            both2(g, d).wait_send()
            pass1(g, d).wait_send()
            for h in range(2):
                own1(g, d, h).wait_send()
                own2(g, d, h).wait_send()
                for e in range(1, 4):
                    line2(g, d, e, h).wait_send()
            for e in range(4):
                pass2(g, d, e).wait_send()
    for j in range(1, n):
        tell(j).wait_send()


def local(activations, cotangent, weight, row_state, column_state):
    tokens, width = activations.shape
    shard, ff = weight.shape
    q = shard // 4
    lanes = ff // 128
    dma = pltpu.SemaphoreType.DMA
    anywhere = pl.BlockSpec(memory_space=pl.ANY)
    vmem = pl.BlockSpec(memory_space=pltpu.VMEM)
    new_weight, row_moment, column_moment = pl.pallas_call(
        kernel,
        out_shape=(
            jax.ShapeDtypeStruct((width, ff), BF16),
            jax.ShapeDtypeStruct((4, q), F32),
            jax.ShapeDtypeStruct((lanes, 128), F32),
        ),
        in_specs=[anywhere, anywhere, anywhere, vmem, vmem],
        out_specs=(anywhere, vmem, vmem),
        scratch_shapes=[
            pltpu.VMEM((SLOTS, 2, tokens, 2 * q), BF16),
            pltpu.VMEM((tokens, ff), BF16),
            pltpu.VMEM((shard, ff), BF16),
            pltpu.VMEM((2, 4, 4, 2, q, ff), BF16),
            pltpu.VMEM((3, 2, 2, 4, q, ff), BF16),
            pltpu.VMEM((3, 2, 2, q, ff), BF16),
            pltpu.VMEM((4, q, ff), F32),
            pltpu.VMEM((4, q, ff), BF16),
            pltpu.VMEM((16, 128), F32),
            pltpu.VMEM((16, 16, 128), F32),
            dma((SLOTS, 2)), dma, dma, dma((4,)),
            dma((3, 2, 2, 4)), dma((3, 2, 2, 4)),
            dma((3, 2, 2)), dma((3, 2, 2)),
            dma((16,)), dma((16,)),
            dma((2, 2, 2)), dma((2, 2, 2)),
            dma((2, 2)), dma((2, 2)),
            dma((2, 2, 4, 2)), dma((2, 2, 4, 2)),
            dma((2, 2, 4)), dma((2, 2, 4)),
        ],
        compiler_params=pltpu.CompilerParams(
            collective_id=0, has_side_effects=True, vmem_limit_bytes=40 * 1024 * 1024
        ),
        cost_estimate=pl.CostEstimate(
            flops=2 * tokens * width * ff,
            bytes_accessed=2 * (tokens * (width + ff) + width * ff),
            transcendentals=shard,
        ),
    )(
        activations, cotangent, weight,
        row_state.reshape(4, q), column_state.reshape(lanes, 128),
    )
    return new_weight, row_moment.reshape(shard), column_moment.reshape(ff)


def solution(mesh):
    in_specs = (
        P(("section", "dp"), None),
        P(("section", "dp"), None),
        P(("section", "dp"), None),
        P(("section", "dp")),
        P("section"),
    )
    out_specs = (P("section", None), P(("section", "dp")), P("section"))
    return jax.shard_map(local, mesh=mesh, in_specs=in_specs, out_specs=out_specs, check_vma=False)
```

time: 283 us -> 121 us (0.43)
  waiting for transfers between devices: 156 us -> 0 us
  Pallas kernels: 0 us -> 104 us
  blocking collectives: 74.8 us -> 0 us
  matrix products: 20.1 us -> 0 us
  between operations: 15.4 us -> 0.66 us
  local copies, waits for them, and re-layouts: 8.7 us -> 15.5 us
  other arithmetic: 6.27 us -> 0 us
    pallas_call x0 -> x1, Pallas kernels: none -> 104 us  [local(): pl.pallas_call(kernel, out_shape=(jax.ShapeDtypeStruct((width, ff), BF16)...]
    reduce_scatter x1 -> x0, waiting for transfers between devices: 87.6 us -> none  [local(): lax.psum_scatter(lax.dot_general(activations, cotangent, (((0,), (0,)), (...]
    psum x2 -> x0, blocking collectives: 74.8 us -> none  [the longest x1 38.8 us: local(): column_sum, row_sum = lax.psum((column_part, row_part), 'dp')]
    all_gather x1 -> x0, waiting for transfers between devices: 68.7 us -> none  [local(): new_weight = lax.all_gather(fresh, 'dp', axis=0, tiled=True)]
    dot_general x1 -> x0, matrix products: 20.1 us -> none  [local(): lax.dot_general(activations, cotangent, (((0,), (0,)), ((), ())), preferr...]
    unnamed x13, local copies, waits for them, and re-layouts: 8.7 us -> 15.5 us
    reduce_sum x3 -> x0, other arithmetic: 4.03 us -> none  [the longest x1 2.12 us: local(): jnp.sum(update * update)]
  transfers between devices with their start and end apart: 2 -> 0, of which waited for: 2 -> 0; matrix products, arithmetic and copies ran while one was open for 0% -> 0% of each run, Pallas kernels for 0% -> 0%
where the time goes in v1:
time: 121 us; the launch traced here: 120 us
  Pallas kernels  104 us (86%)
  local copies, waits for them, and re-layouts  15.5 us (13%)
    pallas_call x1, Pallas kernels, local(): pl.pallas_call(kernel, out_shape=(jax.ShapeDtypeStruct((width, ff), BF16)...  104 us
    unnamed x13, local copies, waits for them, and re-layouts  15.5 us

profile of v1, /device:TPU:0, one launch (start us, length us, event | category | flops | bytes accessed | tf_op | source)
XLA Modules:
  0.0 119.9 jit_solution(13776298165058097075)
XLA Ops:
  0.6 0.0 copy-start.1
  0.6 1.4 %copy-done.1 = bf16[1536,512]{1,0:T(8,128)(2,1)S(1)} copy-done((bf16[1536,512]{1,0:T(8,128)(2,1)S(1)}, bf16[1536,512]{1,0:T(8,128)(2,1)}, u32[]{:S(2)}) %copy-start.1) | copy-done | bytes 1572888
  2.0 0.0 copy-start.2
  2.0 1.0 copy-done.2
  3.1 0.0 copy-start.3
  3.1 0.7 copy-done.3
  3.8 0.0 copy-start.4
  3.8 0.7 copy-done.4
  4.4 103.7 %shard_map.76 = (bf16[8192,512]{1,0:T(8,128)(2,1)S(1)}, f32[4,128]{1,0:T(4,128)S(1)}, f32[4,128]{1,0:T(4,128)S(1)}) custom-call(bf16[1536,8192]{1,0:T(8,128)(2,1)} %act.1, bf16[1536,512]{1,0:T(8,128)(2,1)S(1)} %copy-done.1, bf16[512,512]{1,0:T(8,128)(2,1)S(1)} %copy-done.2, f32[4,128]{1,0:T(4,128)S(1)} %bitcast.6, f32[4,128]{1,0:T(4,128)S(1)} %bitcast.7), custom_call_target="tpu_custom_call" | custom-call | flops 12884901888 | bytes 35127296 | tf_op jit(solution)/shard_map/pallas_call | solution.py:322
  108.1 0.0 copy-start
  108.2 3.2 %copy-done = bf16[8192,512]{1,0:T(8,128)(2,1)} copy-done((bf16[8192,512]{1,0:T(8,128)(2,1)}, bf16[8192,512]{1,0:T(8,128)(2,1)S(1)}, u32[]{:S(2)}) %copy-start) | copy-done | bytes 8388632
  111.4 7.3 %copy.11 = bf16[8192,512]{1,0:T(8,128)(2,1)} copy(bf16[8192,512]{1,0:T(8,128)(2,1)} %copy-done) | data formatting | bytes 16777216
  118.7 0.6 copy.12
  119.3 0.6 copy.13
Async XLA Ops:
  0.6 1.4 %copy-start.1 = (bf16[1536,512]{1,0:T(8,128)(2,1)S(1)}, bf16[1536,512]{1,0:T(8,128)(2,1)}, u32[]{:S(2)}) copy-start(bf16[1536,512]{1,0:T(8,128)(2,1)} %cot.1) | copy-start | bytes 4718596
  2.0 1.0 copy-start.2
  3.1 0.7 copy-start.3
  3.8 0.7 copy-start.4
  108.1 3.2 %copy-start = (bf16[8192,512]{1,0:T(8,128)(2,1)}, bf16[8192,512]{1,0:T(8,128)(2,1)S(1)}, u32[]{:S(2)}) copy-start(bf16[8192,512]{1,0:T(8,128)(2,1)S(1)} %get-tuple-element.12) | copy-start | bytes 25165828

commit v2 on v1

--- a/solution.py
+++ b/solution.py
@@ -15,6 +15,9 @@
 SIDE = 4
 FAR, NEXT, LAST, OWN = 0, 1, 2, 3
 SLOTS = 3
+SHIFT = 12
+PACE = 8
+PIECES = 4
 F32 = jnp.float32
 BF16 = jnp.bfloat16
 
@@ -24,14 +27,17 @@
 
 
 def kernel(
-    act, cot, weight, row_state, col_state,
+    act, cot, weight, row_in, col_in,
     out, row_out, col_out,
-    abuf, cbuf, wbuf, grad, r1, r2, norm, fresh, msg, heard,
-    a_sem, c_sem, w_sem, o_sem,
+    row_state, col_state, abuf, cbuf, wbuf, grad, r1, r2, norm, fresh, msg, heard,
+    go_sem, a_sem, c_sem, w_sem, i_sem, o_sem,
     s1, v1, s2, v2, ss, vs, g1s, g1v, f1s, f1v, g2s, g2v, f2s, f2v,
 ):
     me = lax.axis_index("dp")
     px, pz = me // SIDE, me % SIDE
+    section = lax.axis_index("section")
+    late = 1 - section % 2
+    twin = section + 1 - 2 * (section % 2)
     n = SIDE * SIDE
     q, ff = grad.shape[4], grad.shape[5]
     shard = 4 * q
@@ -49,27 +55,41 @@
 
     step = (1, SIDE - 1)
 
+    def turn(i):
+        i = (i + late * SHIFT) % (SIDE * SIDE)
+        part = i // SIDE
+        near = ((part + 1) // 2) % 2
+        k = near * (NEXT + i % 2) + (part // OWN) * OWN
+        return k, near * ((i - SIDE) // 2) + (1 - near) * (i % SIDE)
+
     def fetch(i, g):
-        k, m = i // SIDE, i % SIDE
+        k, m = turn(i)
         col = place(g, offset(k), offset(m)) * shard + g * 2 * q
         return pltpu.make_async_copy(
             act.at[:, pl.ds(pl.multiple_of(col, 2 * q), 2 * q)],
-            abuf.at[i % SLOTS, g], a_sem.at[i % SLOTS, g],
+            abuf.at[i % SLOTS, :, pl.ds(g * 2 * q, 2 * q)], a_sem.at[i % SLOTS, g],
         )
 
     barrier = pltpu.get_barrier_semaphore()
-    for j in range(1, n):
+    for dx, dz in ((1, 0), (SIDE - 1, 0), (0, 1), (0, SIDE - 1)):
         pl.semaphore_signal(
-            barrier, inc=1, device_id={"dp": (me + j) % n}, device_id_type=MESH
+            barrier, inc=1, device_id={"dp": place(0, dx, dz)}, device_id_type=MESH
         )
+    pl.semaphore_signal(barrier, inc=1, device_id={"section": twin}, device_id_type=MESH)
     get_cot = pltpu.make_async_copy(cot, cbuf, c_sem)
     get_cot.start()
-    for i in range(SLOTS - 1):
+    for g in range(2):
+        fetch(0, g).start()
+    get_cot.wait()
+    for i in range(1, SLOTS - 1):
         for g in range(2):
             fetch(i, g).start()
     get_weight = pltpu.make_async_copy(weight, wbuf, w_sem)
     get_weight.start()
-    get_cot.wait()
+    get_rows = pltpu.make_async_copy(row_in, row_state, i_sem.at[0])
+    get_rows.start()
+    get_cols = pltpu.make_async_copy(col_in, col_state, i_sem.at[1])
+    get_cols.start()
 
     def far1(g, d, m):
         return send(grad.at[g, FAR, m, d], r1.at[0, g, d, m],
@@ -85,24 +105,34 @@
 
     @pl.loop(0, SIDE * SIDE)
     def _(i):
-        k, m = i // SIDE, i % SIDE
+        k, m = turn(i)
         for g in range(2):
             fetch(i, g).wait()
 
-            @pl.when(i + SLOTS - 1 < SIDE * SIDE)
-            def _():
+        @pl.when(i + SLOTS - 1 < SIDE * SIDE)
+        def _():
+            for g in range(2):
                 fetch(i + SLOTS - 1, g).start()
 
-            part = lax.dot_general(
-                abuf[i % SLOTS, g], cbuf[...], (((0,), (0,)), ((), ())),
-                preferred_element_type=F32,
-            ).astype(BF16)
-            grad[g, k, m, 0] = part[:q]
-            grad[g, k, m, 1] = part[q:]
+        part = lax.dot_general(
+            abuf[i % SLOTS], cbuf[...], (((0,), (0,)), ((), ())),
+            preferred_element_type=F32,
+        ).astype(BF16)
+        for g in range(2):
+            for h in range(2):
+                grad[g, k, m, h] = part[(2 * g + h) * q:(2 * g + h + 1) * q]
 
         @pl.when(i == 0)
         def _():
-            pl.semaphore_wait(barrier, n - 1)
+            pl.semaphore_wait(barrier, 5)
+
+        @pl.when((1 - late) * i == PACE)
+        def _():
+            pl.semaphore_signal(go_sem, inc=1, device_id={"section": twin}, device_id_type=MESH)
+
+        @pl.when(late * i == SIDE * SIDE - SHIFT)
+        def _():
+            pl.semaphore_wait(go_sem, 1)
 
         @pl.when(k == FAR)
         def _():
@@ -110,25 +140,21 @@
                 for d in range(2):
                     far1(g, d, m).start()
 
-        @pl.when(k == NEXT)
-        def _():
-            for g in range(2):
-                near1(g, 0, m).start()
-
-        @pl.when(k == LAST)
-        def _():
-            for g in range(2):
-                near1(g, 1, m).start()
-
-    @pl.loop(0, SIDE)
-    def _(m):
-        for g in range(2):
-            for d in range(2):
-                far1(g, d, m).wait_recv()
-                grad[g, NEXT + d, m, d] = (
-                    grad[g, NEXT + d, m, d].astype(F32) + r1[0, g, d, m].astype(F32)
-                ).astype(BF16)
-                both1(g, d, m).start()
+        for d in range(2):
+            @pl.when(k == NEXT + d)
+            def _():
+                for g in range(2):
+                    near1(g, d, m).start()
+
+        for d in range(2):
+            @pl.when(k == NEXT + d)
+            def _():
+                for g in range(2):
+                    far1(g, d, m).wait_recv()
+                    grad[g, NEXT + d, m, d] = (
+                        grad[g, NEXT + d, m, d].astype(F32) + r1[0, g, d, m].astype(F32)
+                    ).astype(BF16)
+                    both1(g, d, m).start()
 
     def total1(g, m, h):
         both1(g, h, m).wait_recv()
@@ -165,6 +191,10 @@
                 grad[g, OWN, NEXT + d, d].astype(F32) + r2[0, g, d].astype(F32)
             ).astype(BF16)
             both2(g, d).start()
+
+    get_rows.wait()
+    get_cols.wait()
+    get_weight.wait()
 
     eye = lax.broadcasted_iota(jnp.int32, (q, q), 0) == lax.broadcasted_iota(jnp.int32, (q, q), 1)
     square_sum = jnp.zeros((1, ff), F32)
@@ -245,7 +275,6 @@
         return send(block, block, f2s.at[g, d, e], f2v.at[g, d, e], place(g, step[d], 0))
 
     keep = []
-    get_weight.wait()
     for h in range(2):
         for g in range(2):
             i = 2 * g + h
@@ -260,27 +289,26 @@
             own2(g, 1, h).start()
             keep.append(pltpu.make_async_copy(fresh.at[i], rows(me, g, h), o_sem.at[i]))
             keep[-1].start()
-    for h in range(2):
+    for own in (True, False):
+        for d in range(2):
+            h = d if own else 1 - d
+            for g in range(2):
+                own1(g, d, h).wait_recv()
+                if own:
+                    pass1(g, d).start()
+                line2(g, 0, 2 - d, h).start()
+                line2(g, 1, 2 - d, h).start()
+    for g in range(2):
+        for h in range(2):
+            pass1(g, h).wait_recv()
+            line2(g, h, 3, h).start()
+    for g in range(2):
+        for h in range(2):
+            line2(g, 1 - h, 3, h).start()
+    for e in range(4):
         for g in range(2):
             for d in range(2):
-                own1(g, 1 - d, h).wait_recv()
-                if h == 1 - d:
-                    pass1(g, 1 - d).start()
-                line2(g, 0, 1 + d, h).start()
-                line2(g, 1, 1 + d, h).start()
-    for e in (0, 1, 2, 3):
-        if e == 3:
-            for g in range(2):
-                for h in range(2):
-                    pass1(g, h).wait_recv()
-                    line2(g, 0, 3, h).start()
-                    line2(g, 1, 3, h).start()
-        for g in range(2):
-            for d in range(2):
-                if e == 0:
-                    own2(g, d, d).wait_recv()
-                else:
-                    line2(g, d, e, d).wait_recv()
+                (own2(g, d, d) if e == 0 else line2(g, d, e, d)).wait_recv()
                 pass2(g, d, e).start()
 
     for e in range(4):
@@ -311,6 +339,22 @@
         tell(j).wait_send()
 
 
+def store(new, row, col, new_out, row_out, col_out, sem):
+    span = new.shape[0] // PIECES
+    copies = [
+        pltpu.make_async_copy(
+            new.at[pl.ds(i * span, span)], new_out.at[pl.ds(i * span, span)], sem.at[i]
+        )
+        for i in range(PIECES)
+    ]
+    copies.append(pltpu.make_async_copy(row, row_out, sem.at[PIECES]))
+    copies.append(pltpu.make_async_copy(col, col_out, sem.at[PIECES + 1]))
+    for copy in copies:
+        copy.start()
+    for copy in copies:
+        copy.wait()
+
+
 def local(activations, cotangent, weight, row_state, column_state):
     tokens, width = activations.shape
     shard, ff = weight.shape
@@ -318,18 +362,21 @@
     lanes = ff // 128
     dma = pltpu.SemaphoreType.DMA
     anywhere = pl.BlockSpec(memory_space=pl.ANY)
+    hbm = pl.BlockSpec(memory_space=pltpu.HBM)
     vmem = pl.BlockSpec(memory_space=pltpu.VMEM)
     new_weight, row_moment, column_moment = pl.pallas_call(
         kernel,
         out_shape=(
-            jax.ShapeDtypeStruct((width, ff), BF16),
+            pltpu.VMEM((width, ff), BF16),
             jax.ShapeDtypeStruct((4, q), F32),
             jax.ShapeDtypeStruct((lanes, 128), F32),
         ),
-        in_specs=[anywhere, anywhere, anywhere, vmem, vmem],
-        out_specs=(anywhere, vmem, vmem),
+        in_specs=[hbm] * 5,
+        out_specs=(vmem, vmem, vmem),
         scratch_shapes=[
-            pltpu.VMEM((SLOTS, 2, tokens, 2 * q), BF16),
+            pltpu.VMEM((4, q), F32),
+            pltpu.VMEM((lanes, 128), F32),
+            pltpu.VMEM((SLOTS, tokens, 4 * q), BF16),
             pltpu.VMEM((tokens, ff), BF16),
             pltpu.VMEM((shard, ff), BF16),
             pltpu.VMEM((2, 4, 4, 2, q, ff), BF16),
@@ -339,7 +386,8 @@
             pltpu.VMEM((4, q, ff), BF16),
             pltpu.VMEM((16, 128), F32),
             pltpu.VMEM((16, 16, 128), F32),
-            dma((SLOTS, 2)), dma, dma, dma((4,)),
+            pltpu.SemaphoreType.REGULAR,
+            dma((SLOTS, 2)), dma, dma, dma((2,)), dma((4,)),
             dma((3, 2, 2, 4)), dma((3, 2, 2, 4)),
             dma((3, 2, 2)), dma((3, 2, 2)),
             dma((16,)), dma((16,)),
@@ -356,10 +404,28 @@
             bytes_accessed=2 * (tokens * (width + ff) + width * ff),
             transcendentals=shard,
         ),
-    )(
-        activations, cotangent, weight,
-        row_state.reshape(4, q), column_state.reshape(lanes, 128),
-    )
+    )(*(
+        pltpu.with_memory_space_constraint(array, pltpu.HBM)
+        for array in (
+            activations, cotangent, weight,
+            row_state.reshape(4, q), column_state.reshape(lanes, 128),
+        )
+    ))
+    new_weight, row_moment, column_moment = pl.pallas_call(
+        store,
+        out_shape=(
+            jax.ShapeDtypeStruct((width, ff), BF16),
+            jax.ShapeDtypeStruct((4, q), F32),
+            jax.ShapeDtypeStruct((lanes, 128), F32),
+        ),
+        in_specs=[vmem] * 3,
+        out_specs=(hbm, hbm, hbm),
+        scratch_shapes=[dma((PIECES + 2,))],
+        compiler_params=pltpu.CompilerParams(vmem_limit_bytes=4 * 1024 * 1024),
+    )(*(
+        pltpu.with_memory_space_constraint(array, pltpu.VMEM)
+        for array in (new_weight, row_moment, column_moment)
+    ))
     return new_weight, row_moment.reshape(shard), column_moment.reshape(ff)
 
 

time: 121 us -> 101 us (0.83)
  local copies, waits for them, and re-layouts: 15.5 us -> 0 us
  Pallas kernels: 104 us -> 99.8 us
    unnamed x13 -> x0, local copies, waits for them, and re-layouts: 15.5 us -> none
    pallas_call x1 -> x2, Pallas kernels: 104 us -> 99.8 us  [the longest x1 96.4 us: local(): pl.pallas_call(kernel, out_shape=(pltpu.VMEM((width, ff), BF16), jax.Shap...]
where the time goes in v2:
time: 101 us; the launch traced here: 100 us
  Pallas kernels  99.8 us (99%)
    pallas_call x1, Pallas kernels, local(): pl.pallas_call(kernel, out_shape=(pltpu.VMEM((width, ff), BF16), jax.Shap...  96.4 us
    pallas_call x1, Pallas kernels, local(): pl.pallas_call(store, out_shape=(jax.ShapeDtypeStruct((width, ff), BF16),...  3.39 us

profile of v2, /device:TPU:0, one launch (start us, length us, event | category | flops | bytes accessed | tf_op | source)
XLA Modules:
  0.0 100.4 jit_solution(5656601685705954477)
XLA Ops:
  0.6 96.4 %shard_map.76 = (bf16[8192,512]{1,0:T(8,128)(2,1)S(1)}, f32[4,128]{1,0:T(4,128)S(1)}, f32[4,128]{1,0:T(4,128)S(1)}) custom-call(bf16[1536,8192]{1,0:T(8,128)(2,1)} %act.1, bf16[1536,512]{1,0:T(8,128)(2,1)} %cot.1, bf16[512,512]{1,0:T(8,128)(2,1)} %weight.1, f32[4,128]{1,0:T(4,128)} %bitcast.4, f32[4,128]{1,0:T(4,128)} %bitcast.5), custom_call_target="tpu_custom_call" | custom-call | flops 12884901888 | bytes 35127296 | tf_op jit(solution)/shard_map/pallas_call | solution.py:367
  97.0 3.4 %shard_map.77 = (bf16[8192,512]{1,0:T(8,128)(2,1)}, f32[4,128]{1,0:T(4,128)}, f32[4,128]{1,0:T(4,128)}) custom-call(bf16[8192,512]{1,0:T(8,128)(2,1)S(1)} %get-tuple-element.9.new, f32[4,128]{1,0:T(4,128)S(1)} %get-tuple-element.10.row, f32[4,128]{1,0:T(4,128)S(1)} %get-tuple-element.11.col), custom_call_target="tpu_custom_call" | custom-call | tf_op jit(solution)/shard_map/pallas_call | solution.py:414

commit v3 on v2

--- a/solution.py
+++ b/solution.py
@@ -30,8 +30,8 @@
     act, cot, weight, row_in, col_in,
     out, row_out, col_out,
     row_state, col_state, abuf, cbuf, wbuf, grad, r1, r2, norm, fresh, msg, heard,
-    go_sem, a_sem, c_sem, w_sem, i_sem, o_sem,
-    s1, v1, s2, v2, ss, vs, g1s, g1v, f1s, f1v, g2s, g2v, f2s, f2v,
+    go_sem, first_sem, a_sem, w_sem, i_sem, o_sem,
+    s1, v1, s2, v2, ss, vs, g1s, g1v, f1s, f1v, g2s, g2v, f2s, f2v, last_v,
 ):
     me = lax.axis_index("dp")
     px, pz = me // SIDE, me % SIDE
@@ -55,6 +55,9 @@
 
     step = (1, SIDE - 1)
 
+    def wait_for(like, sem):
+        pltpu.make_async_copy(like, like, sem).wait()
+
     def turn(i):
         i = (i + late * SHIFT) % (SIDE * SIDE)
         part = i // SIDE
@@ -62,13 +65,16 @@
         k = near * (NEXT + i % 2) + (part // OWN) * OWN
         return k, near * ((i - SIDE) // 2) + (1 - near) * (i % SIDE)
 
-    def fetch(i, g):
+    def fetch_refs(i, g):
         k, m = turn(i)
         col = place(g, offset(k), offset(m)) * shard + g * 2 * q
-        return pltpu.make_async_copy(
+        return (
             act.at[:, pl.ds(pl.multiple_of(col, 2 * q), 2 * q)],
-            abuf.at[i % SLOTS, :, pl.ds(g * 2 * q, 2 * q)], a_sem.at[i % SLOTS, g],
+            abuf.at[i % SLOTS, :, pl.ds(g * 2 * q, 2 * q)],
         )
+
+    def fetch(i, g):
+        return pltpu.make_async_copy(*fetch_refs(i, g), a_sem.at[i % SLOTS])
 
     barrier = pltpu.get_barrier_semaphore()
     for dx, dz in ((1, 0), (SIDE - 1, 0), (0, 1), (0, SIDE - 1)):
@@ -76,12 +82,9 @@
             barrier, inc=1, device_id={"dp": place(0, dx, dz)}, device_id_type=MESH
         )
     pl.semaphore_signal(barrier, inc=1, device_id={"section": twin}, device_id_type=MESH)
-    get_cot = pltpu.make_async_copy(cot, cbuf, c_sem)
+    get_cot = pltpu.make_async_copy(cot, cbuf, first_sem)
     get_cot.start()
-    for g in range(2):
-        fetch(0, g).start()
-    get_cot.wait()
-    for i in range(1, SLOTS - 1):
+    for i in range(SLOTS - 1):
         for g in range(2):
             fetch(i, g).start()
     get_weight = pltpu.make_async_copy(weight, wbuf, w_sem)
@@ -93,27 +96,29 @@
 
     def far1(g, d, m):
         return send(grad.at[g, FAR, m, d], r1.at[0, g, d, m],
-                    s1.at[0, g, d, m], v1.at[0, g, d, m], place(g, step[d], 0))
+                    s1, v1.at[0, g, d, m], place(g, step[d], 0))
 
     def near1(g, d, m):
         return send(grad.at[g, NEXT + d, m, 1 - d], r1.at[1, g, d, m],
-                    s1.at[1, g, d, m], v1.at[1, g, d, m], place(g, step[d], 0))
+                    s1, v1.at[1, g, 1 - d, m], place(g, step[d], 0))
 
     def both1(g, d, m):
         return send(grad.at[g, NEXT + d, m, d], r1.at[2, g, d, m],
-                    s1.at[2, g, d, m], v1.at[2, g, d, m], place(g, step[d], 0))
+                    s1, v1.at[1, g, d, m], place(g, step[d], 0))
 
     @pl.loop(0, SIDE * SIDE)
     def _(i):
         k, m = turn(i)
-        for g in range(2):
-            fetch(i, g).wait()
-
         @pl.when(i + SLOTS - 1 < SIDE * SIDE)
         def _():
             for g in range(2):
                 fetch(i + SLOTS - 1, g).start()
 
+        @pl.when(i == 0)
+        def _():
+            get_cot.wait()
+
+        wait_for(abuf.at[0], a_sem.at[i % SLOTS])
         part = lax.dot_general(
             abuf[i % SLOTS], cbuf[...], (((0,), (0,)), ((), ())),
             preferred_element_type=F32,
@@ -157,23 +162,22 @@
                     both1(g, d, m).start()
 
     def total1(g, m, h):
-        both1(g, h, m).wait_recv()
-        near1(g, 1 - h, m).wait_recv()
+        wait_for(grad.at[g, OWN, m], v1.at[1, g, h, m])
         return (
             grad[g, OWN, m, h].astype(F32) + r1[2, g, h, m].astype(F32)
         ) + r1[1, g, 1 - h, m].astype(F32)
 
     def far2(g, d):
         return send(grad.at[g, OWN, FAR, d], r2.at[0, g, d],
-                    s2.at[0, g, d], v2.at[0, g, d], place(g, 0, step[d]))
+                    s2, v2.at[0, g, d], place(g, 0, step[d]))
 
     def near2(g, d):
         return send(grad.at[g, OWN, NEXT + d, 1 - d], r2.at[1, g, d],
-                    s2.at[1, g, d], v2.at[1, g, d], place(g, 0, step[d]))
+                    s2, v2.at[1, g, 1 - d], place(g, 0, step[d]))
 
     def both2(g, d):
         return send(grad.at[g, OWN, NEXT + d, d], r2.at[2, g, d],
-                    s2.at[2, g, d], v2.at[2, g, d], place(g, 0, step[d]))
+                    s2, v2.at[1, g, d], place(g, 0, step[d]))
 
     for g in range(2):
         for h in range(2):
@@ -204,8 +208,7 @@
         for h in range(2):
             i = 2 * g + h
             mine = total1(g, OWN, h)
-            both2(g, h).wait_recv()
-            near2(g, 1 - h).wait_recv()
+            wait_for(grad.at[g, OWN, OWN], v2.at[1, g, h])
             mine = (mine + r2[2, g, h].astype(F32)) + r2[1, g, 1 - h].astype(F32)
             squares = mine * mine + epsilon_one
             state = jnp.sum(jnp.where(eye, row_state[i:i + 1, :], 0.0), axis=1, keepdims=True)
@@ -225,17 +228,12 @@
     msg[2 * lanes:2 * lanes + 1, :] = jnp.broadcast_to(row_sum, (1, 128))
 
     def tell(j):
-        return send(msg, heard.at[me], ss.at[j], vs.at[me], (me + j) % n)
-
-    def hear(j):
-        other = (me + j) % n
-        return send(msg, heard.at[other], ss.at[0], vs.at[other], other)
+        return send(msg, heard.at[me], ss, vs, (me + j) % n)
 
     for j in range(1, n):
         tell(j).start()
     heard[me] = msg[...]
-    for j in range(1, n):
-        hear(j).wait_recv()
+    wait_for(heard.at[pl.ds(0, n - 1)], vs)
     total = heard[0]
     for j in range(1, n):
         total = total + heard[j]
@@ -254,27 +252,26 @@
 
     def own1(g, d, h):
         return send(fresh.at[2 * g + h], rows(me, g, h),
-                    g1s.at[g, d, h], g1v.at[g, d, h], place(g, 0, step[d]))
+                    g1s, g1v.at[g, d, h], place(g, 0, step[d]))
 
     def own2(g, d, h):
         return send(fresh.at[2 * g + h], rows(me, g, h),
-                    g2s.at[g, d, 0, h], g2v.at[g, d, 0, h], place(g, step[d], 0))
+                    g2s, g2v.at[g, d, 0] if h == d else last_v, place(g, step[d], 0))
 
     def pass1(g, d):
         block = rows(place(g, 0, step[1 - d]), g, d)
-        return send(block, block, f1s.at[g, d], f1v.at[g, d], place(g, 0, step[d]))
+        return send(block, block, f1s, f1v.at[g, d], place(g, 0, step[d]))
 
     away = (0, 1, 3, 2)
 
     def line2(g, d, e, h):
         block = rows(place(g, 0, away[e]), g, h)
-        return send(block, block, g2s.at[g, d, e, h], g2v.at[g, d, e, h], place(g, step[d], 0))
+        return send(block, block, g2s, g2v.at[g, d, e] if h == d else last_v, place(g, step[d], 0))
 
     def pass2(g, d, e):
         block = rows(place(g, step[1 - d], away[e]), g, d)
-        return send(block, block, f2s.at[g, d, e], f2v.at[g, d, e], place(g, step[d], 0))
-
-    keep = []
+        return send(block, block, f2s, f2v, place(g, step[d], 0))
+
     for h in range(2):
         for g in range(2):
             i = 2 * g + h
@@ -287,8 +284,10 @@
             own1(g, 1, h).start()
             own2(g, 0, h).start()
             own2(g, 1, h).start()
-            keep.append(pltpu.make_async_copy(fresh.at[i], rows(me, g, h), o_sem.at[i]))
-            keep[-1].start()
+            pltpu.make_async_copy(fresh.at[i], rows(me, g, h), o_sem).start()
+    wait_for(r1, s1)
+    wait_for(r2, s2)
+    wait_for(heard.at[pl.ds(0, n - 1)], ss)
     for own in (True, False):
         for d in range(2):
             h = d if own else 1 - d
@@ -311,32 +310,13 @@
                 (own2(g, d, d) if e == 0 else line2(g, d, e, d)).wait_recv()
                 pass2(g, d, e).start()
 
-    for e in range(4):
-        for g in range(2):
-            for d in range(2):
-                (own2(g, d, 1 - d) if e == 0 else line2(g, d, e, 1 - d)).wait_recv()
-                pass2(g, d, e).wait_recv()
-    for copy in keep:
-        copy.wait()
-    for g in range(2):
-        for d in range(2):
-            for m in range(SIDE):
-                far1(g, d, m).wait_send()
-                near1(g, d, m).wait_send()
-                both1(g, d, m).wait_send()
-            far2(g, d).wait_send()
-            near2(g, d).wait_send()
-            both2(g, d).wait_send()
-            pass1(g, d).wait_send()
-            for h in range(2):
-                own1(g, d, h).wait_send()
-                own2(g, d, h).wait_send()
-                for e in range(1, 4):
-                    line2(g, d, e, h).wait_send()
-            for e in range(4):
-                pass2(g, d, e).wait_send()
-    for j in range(1, n):
-        tell(j).wait_send()
+    wait_for(fresh, o_sem)
+    wait_for(grad.at[0, 0], g1s)
+    wait_for(r2.at[0], f1s)
+    wait_for(grad.at[0], g2s)
+    wait_for(grad.at[0, 0:2], last_v)
+    wait_for(grad.at[0, 0:2], f2v)
+    wait_for(grad.at[0, 0:2], f2s)
 
 
 def store(new, row, col, new_out, row_out, col_out, sem):
@@ -372,7 +352,7 @@
             jax.ShapeDtypeStruct((lanes, 128), F32),
         ),
         in_specs=[hbm] * 5,
-        out_specs=(vmem, vmem, vmem),
+        out_specs=(anywhere, vmem, vmem),
         scratch_shapes=[
             pltpu.VMEM((4, q), F32),
             pltpu.VMEM((lanes, 128), F32),
@@ -387,14 +367,10 @@
             pltpu.VMEM((16, 128), F32),
             pltpu.VMEM((16, 16, 128), F32),
             pltpu.SemaphoreType.REGULAR,
-            dma((SLOTS, 2)), dma, dma, dma((2,)), dma((4,)),
-            dma((3, 2, 2, 4)), dma((3, 2, 2, 4)),
-            dma((3, 2, 2)), dma((3, 2, 2)),
-            dma((16,)), dma((16,)),
-            dma((2, 2, 2)), dma((2, 2, 2)),
-            dma((2, 2)), dma((2, 2)),
-            dma((2, 2, 4, 2)), dma((2, 2, 4, 2)),
-            dma((2, 2, 4)), dma((2, 2, 4)),
+            dma, dma((SLOTS,)), dma, dma((2,)), dma,
+            dma, dma((2, 2, 2, 4)), dma, dma((2, 2, 2)), dma, dma,
+            dma, dma((2, 2, 2)), dma, dma((2, 2)),
+            dma, dma((2, 2, 4)), dma, dma, dma,
         ],
         compiler_params=pltpu.CompilerParams(
             collective_id=0, has_side_effects=True, vmem_limit_bytes=40 * 1024 * 1024

time: 101 us -> 98.7 us (0.977)
  Pallas kernels: 99.8 us -> 97.9 us
    pallas_call x1, Pallas kernels: 96.4 us -> 94.5 us  [local(): pl.pallas_call(kernel, out_shape=(pltpu.VMEM((width, ff), BF16), jax.Shap...]
where the time goes in v3:
time: 98.7 us; the launch traced here: 98.5 us
  Pallas kernels  97.9 us (99%)
    pallas_call x1, Pallas kernels, local(): pl.pallas_call(kernel, out_shape=(pltpu.VMEM((width, ff), BF16), jax.Shap...  94.5 us
    pallas_call x1, Pallas kernels, local(): pl.pallas_call(store, out_shape=(jax.ShapeDtypeStruct((width, ff), BF16),...  3.39 us

profile of v3, /device:TPU:0, one launch (start us, length us, event | category | flops | bytes accessed | tf_op | source)
XLA Modules:
  0.0 98.5 jit_solution(11506082208041275594)
XLA Ops:
  0.6 94.5 %shard_map.76 = (bf16[8192,512]{1,0:T(8,128)(2,1)S(1)}, f32[4,128]{1,0:T(4,128)S(1)}, f32[4,128]{1,0:T(4,128)S(1)}) custom-call(bf16[1536,8192]{1,0:T(8,128)(2,1)} %act.1, bf16[1536,512]{1,0:T(8,128)(2,1)} %cot.1, bf16[512,512]{1,0:T(8,128)(2,1)} %weight.1, f32[4,128]{1,0:T(4,128)} %bitcast.4, f32[4,128]{1,0:T(4,128)} %bitcast.5), custom_call_target="tpu_custom_call" | custom-call | flops 12884901888 | bytes 35127296 | tf_op jit(solution)/shard_map/pallas_call | solution.py:347
  95.2 3.4 %shard_map.77 = (bf16[8192,512]{1,0:T(8,128)(2,1)}, f32[4,128]{1,0:T(4,128)}, f32[4,128]{1,0:T(4,128)}) custom-call(bf16[8192,512]{1,0:T(8,128)(2,1)S(1)} %get-tuple-element.9.new, f32[4,128]{1,0:T(4,128)S(1)} %get-tuple-element.10.row, f32[4,128]{1,0:T(4,128)S(1)} %get-tuple-element.11.col), custom_call_target="tpu_custom_call" | custom-call | tf_op jit(solution)/shard_map/pallas_call | solution.py:390

commit v4 on v3

--- a/solution.py
+++ b/solution.py
@@ -31,7 +31,7 @@
     out, row_out, col_out,
     row_state, col_state, abuf, cbuf, wbuf, grad, r1, r2, norm, fresh, msg, heard,
     go_sem, first_sem, a_sem, w_sem, i_sem, o_sem,
-    s1, v1, s2, v2, ss, vs, g1s, g1v, f1s, f1v, g2s, g2v, f2s, f2v, last_v,
+    s1, far_v, near_v, s2, v2, ss, vs, g1s, g1v, f1s, f1v, g2s, g2v, f2s, f2v, last_v,
 ):
     me = lax.axis_index("dp")
     px, pz = me // SIDE, me % SIDE
@@ -58,6 +58,8 @@
     def wait_for(like, sem):
         pltpu.make_async_copy(like, like, sem).wait()
 
+    two, four = grad.at[0, 0, 0], grad.at[0, 0, 0:2]
+
     def turn(i):
         i = (i + late * SHIFT) % (SIDE * SIDE)
         part = i // SIDE
@@ -96,15 +98,15 @@
 
     def far1(g, d, m):
         return send(grad.at[g, FAR, m, d], r1.at[0, g, d, m],
-                    s1, v1.at[0, g, d, m], place(g, step[d], 0))
+                    s1, far_v.at[d, m], place(g, step[d], 0))
 
     def near1(g, d, m):
         return send(grad.at[g, NEXT + d, m, 1 - d], r1.at[1, g, d, m],
-                    s1, v1.at[1, g, 1 - d, m], place(g, step[d], 0))
+                    s1, near_v.at[1 - d, m], place(g, step[d], 0))
 
     def both1(g, d, m):
         return send(grad.at[g, NEXT + d, m, d], r1.at[2, g, d, m],
-                    s1, v1.at[1, g, d, m], place(g, step[d], 0))
+                    s1, near_v.at[d, m], place(g, step[d], 0))
 
     @pl.loop(0, SIDE * SIDE)
     def _(i):
@@ -154,43 +156,48 @@
         for d in range(2):
             @pl.when(k == NEXT + d)
             def _():
+                wait_for(two, far_v.at[d, m])
                 for g in range(2):
-                    far1(g, d, m).wait_recv()
                     grad[g, NEXT + d, m, d] = (
                         grad[g, NEXT + d, m, d].astype(F32) + r1[0, g, d, m].astype(F32)
                     ).astype(BF16)
                     both1(g, d, m).start()
 
+    def ready1(m, h):
+        wait_for(four, near_v.at[h, m])
+
     def total1(g, m, h):
-        wait_for(grad.at[g, OWN, m], v1.at[1, g, h, m])
         return (
             grad[g, OWN, m, h].astype(F32) + r1[2, g, h, m].astype(F32)
         ) + r1[1, g, 1 - h, m].astype(F32)
 
     def far2(g, d):
         return send(grad.at[g, OWN, FAR, d], r2.at[0, g, d],
-                    s2, v2.at[0, g, d], place(g, 0, step[d]))
+                    s2, v2.at[0, d], place(g, 0, step[d]))
 
     def near2(g, d):
         return send(grad.at[g, OWN, NEXT + d, 1 - d], r2.at[1, g, d],
-                    s2, v2.at[1, g, 1 - d], place(g, 0, step[d]))
+                    s2, v2.at[1, 1 - d], place(g, 0, step[d]))
 
     def both2(g, d):
         return send(grad.at[g, OWN, NEXT + d, d], r2.at[2, g, d],
-                    s2, v2.at[1, g, d], place(g, 0, step[d]))
-
-    for g in range(2):
-        for h in range(2):
+                    s2, v2.at[1, d], place(g, 0, step[d]))
+
+    for h in range(2):
+        ready1(FAR, h)
+        for g in range(2):
             grad[g, OWN, FAR, h] = total1(g, FAR, h).astype(BF16)
             far2(g, h).start()
     for d in range(2):
-        for g in range(2):
-            for h in range(2):
+        for h in range(2):
+            ready1(NEXT + d, h)
+            for g in range(2):
                 grad[g, OWN, NEXT + d, h] = total1(g, NEXT + d, h).astype(BF16)
+        for g in range(2):
             near2(g, d).start()
     for d in range(2):
-        for g in range(2):
-            far2(g, d).wait_recv()
+        wait_for(two, v2.at[0, d])
+        for g in range(2):
             grad[g, OWN, NEXT + d, d] = (
                 grad[g, OWN, NEXT + d, d].astype(F32) + r2[0, g, d].astype(F32)
             ).astype(BF16)
@@ -204,11 +211,12 @@
     square_sum = jnp.zeros((1, ff), F32)
     update_sum = jnp.zeros((1, ff), F32)
     row_sum = jnp.zeros((1, 1), F32)
-    for g in range(2):
-        for h in range(2):
+    for h in range(2):
+        ready1(OWN, h)
+        wait_for(four, v2.at[1, h])
+        for g in range(2):
             i = 2 * g + h
             mine = total1(g, OWN, h)
-            wait_for(grad.at[g, OWN, OWN], v2.at[1, g, h])
             mine = (mine + r2[2, g, h].astype(F32)) + r2[1, g, 1 - h].astype(F32)
             squares = mine * mine + epsilon_one
             state = jnp.sum(jnp.where(eye, row_state[i:i + 1, :], 0.0), axis=1, keepdims=True)
@@ -252,21 +260,21 @@
 
     def own1(g, d, h):
         return send(fresh.at[2 * g + h], rows(me, g, h),
-                    g1s, g1v.at[g, d, h], place(g, 0, step[d]))
+                    g1s, g1v.at[d, h], place(g, 0, step[d]))
 
     def own2(g, d, h):
         return send(fresh.at[2 * g + h], rows(me, g, h),
-                    g2s, g2v.at[g, d, 0] if h == d else last_v, place(g, step[d], 0))
+                    g2s, g2v.at[d, 0] if h == d else last_v, place(g, step[d], 0))
 
     def pass1(g, d):
         block = rows(place(g, 0, step[1 - d]), g, d)
-        return send(block, block, f1s, f1v.at[g, d], place(g, 0, step[d]))
+        return send(block, block, f1s, f1v.at[d], place(g, 0, step[d]))
 
     away = (0, 1, 3, 2)
 
     def line2(g, d, e, h):
         block = rows(place(g, 0, away[e]), g, h)
-        return send(block, block, g2s, g2v.at[g, d, e] if h == d else last_v, place(g, step[d], 0))
+        return send(block, block, g2s, g2v.at[d, e] if h == d else last_v, place(g, step[d], 0))
 
     def pass2(g, d, e):
         block = rows(place(g, step[1 - d], away[e]), g, d)
@@ -291,23 +299,23 @@
     for own in (True, False):
         for d in range(2):
             h = d if own else 1 - d
+            wait_for(two, g1v.at[d, h])
             for g in range(2):
-                own1(g, d, h).wait_recv()
                 if own:
                     pass1(g, d).start()
                 line2(g, 0, 2 - d, h).start()
                 line2(g, 1, 2 - d, h).start()
-    for g in range(2):
-        for h in range(2):
-            pass1(g, h).wait_recv()
+    for h in range(2):
+        wait_for(two, f1v.at[h])
+        for g in range(2):
             line2(g, h, 3, h).start()
-    for g in range(2):
-        for h in range(2):
+    for h in range(2):
+        for g in range(2):
             line2(g, 1 - h, 3, h).start()
     for e in range(4):
-        for g in range(2):
-            for d in range(2):
-                (own2(g, d, d) if e == 0 else line2(g, d, e, d)).wait_recv()
+        for d in range(2):
+            wait_for(two, g2v.at[d, e])
+            for g in range(2):
                 pass2(g, d, e).start()
 
     wait_for(fresh, o_sem)
@@ -368,9 +376,9 @@
             pltpu.VMEM((16, 16, 128), F32),
             pltpu.SemaphoreType.REGULAR,
             dma, dma((SLOTS,)), dma, dma((2,)), dma,
-            dma, dma((2, 2, 2, 4)), dma, dma((2, 2, 2)), dma, dma,
-            dma, dma((2, 2, 2)), dma, dma((2, 2)),
-            dma, dma((2, 2, 4)), dma, dma, dma,
+            dma, dma((2, 4)), dma((2, 4)), dma, dma((2, 2)), dma, dma,
+            dma, dma((2, 2)), dma, dma((2,)),
+            dma, dma((2, 4)), dma, dma, dma,
         ],
         compiler_params=pltpu.CompilerParams(
             collective_id=0, has_side_effects=True, vmem_limit_bytes=40 * 1024 * 1024

time: 98.7 us -> 98.5 us (level)
  no operation moved by 1% of the time
where the time goes in v4:
time: 98.5 us; the launch traced here: 98.4 us
  Pallas kernels  97.7 us (99%)
    pallas_call x1, Pallas kernels, local(): pl.pallas_call(kernel, out_shape=(pltpu.VMEM((width, ff), BF16), jax.Shap...  94.3 us
    pallas_call x1, Pallas kernels, local(): pl.pallas_call(store, out_shape=(jax.ShapeDtypeStruct((width, ff), BF16),...  3.39 us

profile of v4, /device:TPU:0, one launch (start us, length us, event | category | flops | bytes accessed | tf_op | source)
XLA Modules:
  0.0 98.4 jit_solution(12286509292108620827)
XLA Ops:
  0.6 94.3 %shard_map.76 = (bf16[8192,512]{1,0:T(8,128)(2,1)S(1)}, f32[4,128]{1,0:T(4,128)S(1)}, f32[4,128]{1,0:T(4,128)S(1)}) custom-call(bf16[1536,8192]{1,0:T(8,128)(2,1)} %act.1, bf16[1536,512]{1,0:T(8,128)(2,1)} %cot.1, bf16[512,512]{1,0:T(8,128)(2,1)} %weight.1, f32[4,128]{1,0:T(4,128)} %bitcast.4, f32[4,128]{1,0:T(4,128)} %bitcast.5), custom_call_target="tpu_custom_call" | custom-call | flops 12884901888 | bytes 35127296 | tf_op jit(solution)/shard_map/pallas_call | solution.py:355
  95.0 3.4 %shard_map.77 = (bf16[8192,512]{1,0:T(8,128)(2,1)}, f32[4,128]{1,0:T(4,128)}, f32[4,128]{1,0:T(4,128)}) custom-call(bf16[8192,512]{1,0:T(8,128)(2,1)S(1)} %get-tuple-element.9.new, f32[4,128]{1,0:T(4,128)S(1)} %get-tuple-element.10.row, f32[4,128]{1,0:T(4,128)S(1)} %get-tuple-element.11.col), custom_call_target="tpu_custom_call" | custom-call | tf_op jit(solution)/shard_map/pallas_call | solution.py:398

commit v5 on v4

--- a/solution.py
+++ b/solution.py
@@ -67,16 +67,19 @@
         k = near * (NEXT + i % 2) + (part // OWN) * OWN
         return k, near * ((i - SIDE) // 2) + (1 - near) * (i % SIDE)
 
-    def fetch_refs(i, g):
+    def chunk(k, g, c):
+        near = ((k + 1) // 2) % 2
+        return near * (NEXT + c) + (1 - near) * k, c + near * (LAST - k) * (1 - 2 * c)
+
+    def fetch(i, g, c):
         k, m = turn(i)
-        col = place(g, offset(k), offset(m)) * shard + g * 2 * q
-        return (
-            act.at[:, pl.ds(pl.multiple_of(col, 2 * q), 2 * q)],
-            abuf.at[i % SLOTS, :, pl.ds(g * 2 * q, 2 * q)],
+        kc, h = chunk(k, g, c)
+        col = place(g, offset(kc), offset(m)) * shard + (2 * g + h) * q
+        return pltpu.make_async_copy(
+            act.at[:, pl.ds(pl.multiple_of(col, q), q)],
+            abuf.at[i % SLOTS, :, pl.ds((2 * g + c) * q, q)],
+            a_sem.at[i % SLOTS],
         )
-
-    def fetch(i, g):
-        return pltpu.make_async_copy(*fetch_refs(i, g), a_sem.at[i % SLOTS])
 
     barrier = pltpu.get_barrier_semaphore()
     for dx, dz in ((1, 0), (SIDE - 1, 0), (0, 1), (0, SIDE - 1)):
@@ -88,7 +91,8 @@
     get_cot.start()
     for i in range(SLOTS - 1):
         for g in range(2):
-            fetch(i, g).start()
+            for c in range(2):
+                fetch(i, g, c).start()
     get_weight = pltpu.make_async_copy(weight, wbuf, w_sem)
     get_weight.start()
     get_rows = pltpu.make_async_copy(row_in, row_state, i_sem.at[0])
@@ -114,7 +118,8 @@
         @pl.when(i + SLOTS - 1 < SIDE * SIDE)
         def _():
             for g in range(2):
-                fetch(i + SLOTS - 1, g).start()
+                for c in range(2):
+                    fetch(i + SLOTS - 1, g, c).start()
 
         @pl.when(i == 0)
         def _():
@@ -126,8 +131,9 @@
             preferred_element_type=F32,
         ).astype(BF16)
         for g in range(2):
-            for h in range(2):
-                grad[g, k, m, h] = part[(2 * g + h) * q:(2 * g + h + 1) * q]
+            for c in range(2):
+                kc, h = chunk(k, g, c)
+                grad[g, kc, m, h] = part[(2 * g + c) * q:(2 * g + c + 1) * q]
 
         @pl.when(i == 0)
         def _():
@@ -147,15 +153,15 @@
                 for d in range(2):
                     far1(g, d, m).start()
 
-        for d in range(2):
-            @pl.when(k == NEXT + d)
-            def _():
-                for g in range(2):
+        @pl.when(k == NEXT)
+        def _():
+            for g in range(2):
+                for d in range(2):
                     near1(g, d, m).start()
 
-        for d in range(2):
-            @pl.when(k == NEXT + d)
-            def _():
+        @pl.when(k == LAST)
+        def _():
+            for d in range(2):
                 wait_for(two, far_v.at[d, m])
                 for g in range(2):
                     grad[g, NEXT + d, m, d] = (

time: 98.5 us -> 98.8 us (level)
  no operation moved by 1% of the time
where the time goes in v5:
time: 98.8 us; the launch traced here: 98.7 us
  Pallas kernels  98.1 us (99%)
    pallas_call x1, Pallas kernels, local(): pl.pallas_call(kernel, out_shape=(pltpu.VMEM((width, ff), BF16), jax.Shap...  94.7 us
    pallas_call x1, Pallas kernels, local(): pl.pallas_call(store, out_shape=(jax.ShapeDtypeStruct((width, ff), BF16),...  3.39 us

profile of v5, /device:TPU:0, one launch (start us, length us, event | category | flops | bytes accessed | tf_op | source)
XLA Modules:
  0.0 98.7 jit_solution(13027528948738762322)
XLA Ops:
  0.6 94.7 %shard_map.76 = (bf16[8192,512]{1,0:T(8,128)(2,1)S(1)}, f32[4,128]{1,0:T(4,128)S(1)}, f32[4,128]{1,0:T(4,128)S(1)}) custom-call(bf16[1536,8192]{1,0:T(8,128)(2,1)} %act.1, bf16[1536,512]{1,0:T(8,128)(2,1)} %cot.1, bf16[512,512]{1,0:T(8,128)(2,1)} %weight.1, f32[4,128]{1,0:T(4,128)} %bitcast.4, f32[4,128]{1,0:T(4,128)} %bitcast.5), custom_call_target="tpu_custom_call" | custom-call | flops 12884901888 | bytes 35127296 | tf_op jit(solution)/shard_map/pallas_call | solution.py:361
  95.3 3.4 %shard_map.77 = (bf16[8192,512]{1,0:T(8,128)(2,1)}, f32[4,128]{1,0:T(4,128)}, f32[4,128]{1,0:T(4,128)}) custom-call(bf16[8192,512]{1,0:T(8,128)(2,1)S(1)} %get-tuple-element.9.new, f32[4,128]{1,0:T(4,128)S(1)} %get-tuple-element.10.row, f32[4,128]{1,0:T(4,128)S(1)} %get-tuple-element.11.col), custom_call_target="tpu_custom_call" | custom-call | tf_op jit(solution)/shard_map/pallas_call | solution.py:404
